TPU v7x, 32 devices: a whole 2x2x4 slice. The times are simulated.
32 devices in a mesh: batch: 8 (over z, x), tensor: 4 (over y, core).
Axes of the slice: x: 2, y: 2, z: 4, core: 2. Of those that a mesh axis runs over, the one named last changes fastest.
Arguments:
- tokens: bfloat16 [16384, 512], P('batch', 'tensor'), may hold values from -6 to 6
- cotangent: float32 [16384, 512], P('batch', 'tensor'), may hold values from -6 to 6
- query_weight: bfloat16 [512, 512], P(None, 'tensor'), may hold values from -0.25 to 0.25
- key_weight: bfloat16 [512, 512], P(None, 'tensor'), may hold values from -0.25 to 0.25
- value_weight: bfloat16 [512, 512], P(None, 'tensor'), may hold values from -0.25 to 0.25
- output_weight: bfloat16 [512, 512], P('tensor'), may hold values from -0.75 to 0.75
- up_weight: bfloat16 [512, 2048], P(None, 'tensor'), may hold values from -0.25 to 0.25
- down_weight: bfloat16 [2048, 512], P('tensor'), may hold values from -0.125 to 0.125
- first_gate: bfloat16 [512, 512], P(None, 'tensor'), may hold values from -0.25 to 0.25
- second_gate: bfloat16 [512, 512], P(None, 'tensor'), may hold values from -0.25 to 0.25
- first_bias: float32 [512], P('tensor'), may hold values from -4 to 4
- second_bias: float32 [512], P('tensor'), may hold values from -4 to 4
- first_gain: float32 [512], replicated, may hold values from 0.5 to 1.5
- first_shift: float32 [512], replicated, may hold values from -2 to 2
- second_gain: float32 [512], replicated, may hold values from 0.5 to 1.5
- second_shift: float32 [512], replicated, may hold values from -2 to 2
Outputs:
- layer_output: bfloat16 [16384, 512], P('batch', 'tensor')
- input_gradient: float32 [16384, 512], P('batch', 'tensor')
- query_gradient: float32 [512, 512], P(None, 'tensor')
- key_gradient: float32 [512, 512], P(None, 'tensor')
- value_gradient: float32 [512, 512], P(None, 'tensor')
- output_gradient: float32 [512, 512], P('tensor')
- up_gradient: float32 [512, 2048], P(None, 'tensor')
- down_gradient: float32 [2048, 512], P('tensor')
- first_gate_gradient: float32 [512, 512], P(None, 'tensor')
- second_gate_gradient: float32 [512, 512], P(None, 'tensor')
- first_bias_gradient: float32 [512], P('tensor')
- second_bias_gradient: float32 [512], P('tensor')
- first_gain_gradient: float32 [512], replicated
- first_shift_gradient: float32 [512], replicated
- second_gain_gradient: float32 [512], replicated
- second_shift_gradient: float32 [512], replicated
- gate_stats: float32 [4], replicated
All inputs are finite; a program needn't handle non-finite values.
Results may differ from a plain program's by a relative error of at most 0.012.
Values may be sent and summed in bfloat16 or wider, within the bound.
A program may use at most 128 MiB of HBM per device.

v0:
```python
import math

import jax
import jax.numpy as jnp
from jax import lax
from jax.sharding import PartitionSpec as P

HD = 64
LEN = 1024


EPSILON = 1e-05


def normalize_rows(gathered, gain, shift):
    centred = gathered - jnp.mean(gathered, axis=-1, keepdims=True)
    reciprocal = lax.rsqrt(jnp.mean(centred * centred, axis=-1, keepdims=True) + EPSILON)
    unit_rows = centred * reciprocal
    return (unit_rows * gain + shift, unit_rows, reciprocal)


def smooth(values):
    return jax.nn.gelu(values, approximate=True)


def norm_backward(partial_value, unit_rows, reciprocal, gain, col_start, col_share):
    full_width = partial_value.shape[1]
    unit_own = lax.dynamic_slice_in_dim(unit_rows, col_start, col_share, 1)
    gain_own = lax.dynamic_slice_in_dim(gain, col_start, col_share, 0)
    summed = lax.psum(partial_value, "tensor")
    own_grad = lax.dynamic_slice_in_dim(summed, col_start, col_share, 1)
    scaled_full = summed * gain
    first_mean = jnp.mean(scaled_full, axis=-1, keepdims=True)
    second_mean = jnp.mean(scaled_full * unit_rows, axis=-1, keepdims=True)
    scaled = own_grad * gain_own
    input_part = reciprocal * (scaled - first_mean - unit_own * second_mean)
    zeros_full = jnp.zeros((full_width,), jnp.float32)
    gain_grad = lax.dynamic_update_slice_in_dim(
        zeros_full, jnp.sum(own_grad * unit_own, axis=0), col_start, 0
    )
    shift_grad = lax.dynamic_update_slice_in_dim(
        zeros_full, jnp.sum(own_grad, axis=0), col_start, 0
    )
    return (input_part, gain_grad, shift_grad)


def per_device(
    tokens,
    cotangent,
    query_weight,
    key_weight,
    value_weight,
    output_weight,
    up_weight,
    down_weight,
    first_gate,
    second_gate,
    first_bias,
    second_bias,
    first_gain,
    first_shift,
    second_gain,
    second_shift,
):
    row_count, col_share = tokens.shape
    col_start = lax.axis_index("tensor") * col_share
    window_count = row_count // LEN
    head_count = col_share // HD
    scaling = 1.0 / math.sqrt(HD)
    places = jnp.arange(LEN)
    causal = (places[:, None] >= places[None, :])[None]

    def scores_of(query_rows, key_rows):
        raw = (
            jnp.einsum("qhd,khd->hqk", query_rows, key_rows, preferred_element_type=jnp.float32)
            * scaling
        )
        return jnp.where(causal, raw, -1e30)

    def attend_forward(triple):
        query_rows, key_rows, value_rows = triple
        scores = scores_of(query_rows, key_rows)
        row_peak = jnp.max(scores, axis=-1, keepdims=True)
        expd = jnp.exp(scores - row_peak)
        row_total = jnp.sum(expd, axis=-1, keepdims=True)
        probs = expd / row_total
        output_rows = jnp.einsum(
            "hqk,khd->qhd",
            probs.astype(jnp.bfloat16),
            value_rows,
            preferred_element_type=jnp.float32,
        )
        return (output_rows.astype(jnp.bfloat16), (row_peak + jnp.log(row_total))[..., 0])

    def attend_backward(group):
        query_rows, key_rows, value_rows, grad_rows, logsum = group
        probs = jnp.exp(scores_of(query_rows, key_rows) - logsum[..., None])
        value_grad = jnp.einsum(
            "hqk,qhd->khd",
            probs.astype(jnp.bfloat16),
            grad_rows,
            preferred_element_type=jnp.float32,
        )
        grad_probs = jnp.einsum(
            "qhd,khd->hqk", grad_rows, value_rows, preferred_element_type=jnp.float32
        )
        centre = jnp.sum(grad_probs * probs, axis=-1, keepdims=True)
        grad_scores = (probs * (grad_probs - centre)).astype(jnp.bfloat16)
        query_grad = (
            jnp.einsum("hqk,khd->qhd", grad_scores, key_rows, preferred_element_type=jnp.float32)
            * scaling
        )
        key_grad = (
            jnp.einsum("hqk,qhd->khd", grad_scores, query_rows, preferred_element_type=jnp.float32)
            * scaling
        )
        return (
            query_grad.astype(jnp.bfloat16),
            key_grad.astype(jnp.bfloat16),
            value_grad.astype(jnp.bfloat16),
        )

    def branch_total(partial_value):
        return lax.psum_scatter(partial_value, "tensor", scatter_dimension=1, tiled=True)

    def branch_gradient(piece):
        return lax.all_gather(piece, "tensor", axis=1, tiled=True)

    gathered = lax.all_gather(tokens, "tensor", axis=1, tiled=True).astype(jnp.float32)
    first_normed, first_unit, first_recip = normalize_rows(gathered, first_gain, first_shift)
    first_low = first_normed.astype(jnp.bfloat16)

    def project(weight):
        product = jnp.dot(first_low, weight, preferred_element_type=jnp.float32)
        return product.astype(jnp.bfloat16).reshape(window_count, LEN, head_count, HD)

    queries, keys_here, values_here = (
        project(query_weight),
        project(key_weight),
        project(value_weight),
    )
    attended, logsums = lax.map(attend_forward, (queries, keys_here, values_here))
    attended_flat = attended.reshape(row_count, col_share)
    attn_branch = branch_total(
        jnp.dot(attended_flat, output_weight, preferred_element_type=jnp.float32)
    )
    attn_gate = jax.nn.sigmoid(
        jnp.dot(first_low, first_gate, preferred_element_type=jnp.float32) + first_bias
    )
    middle = tokens.astype(jnp.float32) + attn_gate * attn_branch
    middle_rows = lax.all_gather(middle, "tensor", axis=1, tiled=True)
    second_normed, second_unit, second_recip = normalize_rows(
        middle_rows, second_gain, second_shift
    )
    second_low = second_normed.astype(jnp.bfloat16)
    pre_hidden = jnp.dot(second_low, up_weight, preferred_element_type=jnp.float32)
    hidden, gelu_pullback = jax.vjp(smooth, pre_hidden)
    hidden_low = hidden.astype(jnp.bfloat16)
    ffn_branch = branch_total(jnp.dot(hidden_low, down_weight, preferred_element_type=jnp.float32))
    ffn_gate = jax.nn.sigmoid(
        jnp.dot(second_low, second_gate, preferred_element_type=jnp.float32) + second_bias
    )
    layer_output = (middle + ffn_gate * ffn_branch).astype(jnp.bfloat16)
    grad_ffn_branch = (cotangent * ffn_gate).astype(jnp.bfloat16)
    grad_ffn_logit = (cotangent * ffn_branch * ffn_gate * (1.0 - ffn_gate)).astype(jnp.bfloat16)
    ffn_grad_rows = branch_gradient(grad_ffn_branch)
    down_grad = jnp.einsum(
        "rf,rd->fd", hidden_low, ffn_grad_rows, preferred_element_type=jnp.float32
    )
    grad_hidden = jnp.einsum(
        "rd,fd->rf", ffn_grad_rows, down_weight, preferred_element_type=jnp.float32
    )
    grad_pre = gelu_pullback(grad_hidden)[0].astype(jnp.bfloat16)
    up_grad = jnp.einsum("rd,rf->df", second_low, grad_pre, preferred_element_type=jnp.float32)
    second_gate_grad = jnp.einsum(
        "rd,rc->dc", second_low, grad_ffn_logit, preferred_element_type=jnp.float32
    )
    second_bias_grad = jnp.sum(grad_ffn_logit.astype(jnp.float32), axis=0)
    second_partial = jnp.einsum(
        "rf,df->rd", grad_pre, up_weight, preferred_element_type=jnp.float32
    ) + jnp.einsum("rc,dc->rd", grad_ffn_logit, second_gate, preferred_element_type=jnp.float32)
    middle_part, second_gain_grad, second_shift_grad = norm_backward(
        second_partial, second_unit, second_recip, second_gain, col_start, col_share
    )
    grad_middle = cotangent + middle_part
    grad_attn_branch = (grad_middle * attn_gate).astype(jnp.bfloat16)
    grad_attn_logit = (grad_middle * attn_branch * attn_gate * (1.0 - attn_gate)).astype(
        jnp.bfloat16
    )
    attn_grad_rows = branch_gradient(grad_attn_branch)
    output_grad = jnp.einsum(
        "rc,rd->cd", attended_flat, attn_grad_rows, preferred_element_type=jnp.float32
    )
    grad_attended = jnp.einsum(
        "rd,cd->rc", attn_grad_rows, output_weight, preferred_element_type=jnp.float32
    )
    grad_attended = grad_attended.astype(jnp.bfloat16).reshape(window_count, LEN, head_count, HD)
    query_grads, key_grads, value_grads = lax.map(
        attend_backward, (queries, keys_here, values_here, grad_attended, logsums)
    )
    query_grads = query_grads.reshape(row_count, col_share)
    key_grads = key_grads.reshape(row_count, col_share)
    value_grads = value_grads.reshape(row_count, col_share)

    def weight_grad(piece):
        return jnp.einsum("rd,rc->dc", first_low, piece, preferred_element_type=jnp.float32)

    def input_part(piece, weight):
        return jnp.einsum("rc,dc->rd", piece, weight, preferred_element_type=jnp.float32)

    query_grad, key_grad, value_grad = (
        weight_grad(query_grads),
        weight_grad(key_grads),
        weight_grad(value_grads),
    )
    first_gate_grad = weight_grad(grad_attn_logit)
    first_bias_grad = jnp.sum(grad_attn_logit.astype(jnp.float32), axis=0)
    first_partial = (
        input_part(query_grads, query_weight)
        + input_part(key_grads, key_weight)
        + input_part(value_grads, value_weight)
        + input_part(grad_attn_logit, first_gate)
    )
    first_part, first_gain_grad, first_shift_grad = norm_backward(
        first_partial, first_unit, first_recip, first_gain, col_start, col_share
    )
    input_gradient = grad_middle + first_part
    (
        query_grad,
        key_grad,
        value_grad,
        output_grad,
        up_grad,
        down_grad,
        first_gate_grad,
        second_gate_grad,
        first_bias_grad,
        second_bias_grad,
    ) = lax.psum(
        (
            query_grad,
            key_grad,
            value_grad,
            output_grad,
            up_grad,
            down_grad,
            first_gate_grad,
            second_gate_grad,
            first_bias_grad,
            second_bias_grad,
        ),
        "batch",
    )
    local_sums = jnp.stack(
        [
            jnp.sum(attn_gate),
            jnp.sum(attn_gate * attn_gate),
            jnp.sum(ffn_gate),
            jnp.sum(ffn_gate * ffn_gate),
        ]
    )
    gate_sums, first_gain_grad, first_shift_grad, second_gain_grad, second_shift_grad = lax.psum(
        (local_sums, first_gain_grad, first_shift_grad, second_gain_grad, second_shift_grad),
        ("batch", "tensor"),
    )
    entries = float(row_count * col_share * lax.axis_size("batch") * lax.axis_size("tensor"))
    first_mean = gate_sums[0] / entries
    second_mean = gate_sums[2] / entries
    gate_stats = jnp.stack(
        [
            first_mean,
            gate_sums[1] / entries - first_mean * first_mean,
            second_mean,
            gate_sums[3] / entries - second_mean * second_mean,
        ]
    )
    return (
        layer_output,
        input_gradient,
        query_grad,
        key_grad,
        value_grad,
        output_grad,
        up_grad,
        down_grad,
        first_gate_grad,
        second_gate_grad,
        first_bias_grad,
        second_bias_grad,
        first_gain_grad,
        first_shift_grad,
        second_gain_grad,
        second_shift_grad,
        gate_stats,
    )


def solution(mesh):
    in_specs = (
        P("batch", "tensor"),
        P("batch", "tensor"),
        P(None, "tensor"),
        P(None, "tensor"),
        P(None, "tensor"),
        P("tensor", None),
        P(None, "tensor"),
        P("tensor", None),
        P(None, "tensor"),
        P(None, "tensor"),
        P("tensor"),
        P("tensor"),
        P(),
        P(),
        P(),
        P(),
    )
    out_specs = (
        P("batch", "tensor"),
        P("batch", "tensor"),
        P(None, "tensor"),
        P(None, "tensor"),
        P(None, "tensor"),
        P("tensor", None),
        P(None, "tensor"),
        P("tensor", None),
        P(None, "tensor"),
        P(None, "tensor"),
        P("tensor"),
        P("tensor"),
        P(),
        P(),
        P(),
        P(),
        P(),
    )
    return jax.shard_map(
        per_device, mesh=mesh, in_specs=in_specs, out_specs=out_specs, check_vma=False
    )
```

profile of v0, /device:TPU:0, one launch (start us, length us, event | category | flops | bytes accessed | tf_op | source)
XLA Modules:
  0.0 679.7 jit_solution(14604877847070264445)
XLA Ops:
  8.0 27.2 %all-gather.5.cloned.1.call-done = bf16[2048,512]{1,0:T(8,128)(2,1)} async-done(((bf16[2048,128]{1,0:T(8,128)(2,1)}), bf16[2048,512]{1,0:T(8,128)(2,1)}) %all-gather.5.cloned.1.call-update) | async-done | bytes 2097168 | tf_op jit(solution)/shard_map/all_gather | solution.py:129
  42.9 3.5 copy.53
  52.5 3.2 reshape.177
  55.6 3.5 copy.51
  60.0 17.6 %while.28 = (s32[]{:T(128)}, bf16[2,1024,2,64]{1,3,2,0:T(8,128)(2,1)}, f32[2,2,1024]{2,1,0:T(2,128)S(1)}, bf16[2,1024,2,64]{1,3,2,0:T(8,128)(2,1)}, bf16[2,1024,...) while((s32[]{:T(128)}, bf16[2,1024,2,64]{1,3,2,0:T(8,128)(2,1)}, ...), condition=%wide.region_5.6_spmd.clone, body=%wide.region_2.5_spmd.clone.sunk | while | flops 563214336 | bytes 36767916 | solution.py:142
  60.3 2.8 fusion.169
  69.1 2.8 fusion.169
  74.0 2.8 fusion.171
  83.1 44.4 %reduce-scatter.3.cloned.1.call-done = f32[2048,128]{1,0:T(8,128)} async-done(((f32[2048,512]{1,0:T(8,128)}), f32[2048,128]{1,0:T(8,128)}) %reduce-scatter.3.cloned.1.call-update) | async-done | bytes 1048592 | tf_op jit(solution)/shard_map/reduce_scatter | solution.py:124
  127.5 3.4 multiply_add_fusion.2
  131.0 35.1 %all-gather.7.cloned.1.call-done = f32[2048,512]{1,0:T(8,128)} async-done(((f32[2048,128]{1,0:T(8,128)}), f32[2048,512]{1,0:T(8,128)}) %all-gather.7.cloned.1.call-update) | async-done | bytes 4194320 | tf_op jit(solution)/shard_map/all_gather | solution.py:151
  168.7 3.0 multiply_reduce_fusion.3
  177.8 3.5 fusion.84
  181.4 44.6 %reduce-scatter.5.cloned.1.call-done = f32[2048,128]{1,0:T(8,128)} async-done(((f32[2048,512]{1,0:T(8,128)}), f32[2048,128]{1,0:T(8,128)}) %reduce-scatter.5.cloned.1.call-update) | async-done | bytes 1048592 | tf_op jit(solution)/shard_map/reduce_scatter | solution.py:124
  226.0 4.6 fusion.86
  230.7 22.9 %all-gather.9.cloned.1.call-done = bf16[2048,512]{1,0:T(8,128)(2,1)} async-done(((bf16[2048,128]{1,0:T(8,128)(2,1)}), bf16[2048,512]{1,0:T(8,128)(2,1)}) %all-gather.9.cloned.1.call-update) | async-done | bytes 2097168 | tf_op jit(solution)/shard_map/all_gather | solution.py:127
  253.6 5.6 fusion.74
  263.4 85.5 %all-reduce.7.cloned.1.call-done = f32[2048,512]{1,0:T(8,128)} async-done(((f32[2048,512]{1,0:T(8,128)}), f32[2048,512]{1,0:T(8,128)}) %all-reduce.7.cloned.1.call-update) | async-done | bytes 4194320 | tf_op jit(solution)/shard_map/psum | solution.py:30
  348.9 4.4 multiply_reduce_fusion.5
  353.3 4.6 dynamic-slice_reduce_fusion.1
  361.7 3.8 fusion.98
  365.6 17.4 %all-gather.11.cloned.1.call-done = bf16[2048,512]{1,0:T(8,128)(2,1)} async-done(((bf16[2048,128]{1,0:T(8,128)(2,1)}), bf16[2048,512]{1,0:T(8,128)(2,1)}) %all-gather.11.cloned.1.call-update) | async-done | bytes 2097168 | tf_op jit(solution)/shard_map/all_gather | solution.py:127
  387.4 26.0 %while.29 = (s32[]{:T(128)}, bf16[2,1024,2,64]{1,3,2,0:T(8,128)(2,1)}, bf16[2,1024,2,64]{1,3,2,0:T(8,128)(2,1)S(1)}, bf16[2,1024,2,64]{1,3,2,0:T(8,128)(2,1)S(1)...) while((s32[]{:T(128)}, ...), condition=%wide.region_15.16_spmd.clone, body=%wide.region_13.15_spmd.clone.sunk | while | flops 1375336448 | bytes 73987240 | solution.py:198
  391.6 3.0 multiply_reduce_fusion.11
  404.5 3.0 multiply_reduce_fusion.11
  423.1 5.7 fusion.83
  436.2 22.0 %all-reduce.1 = (f32[128]{0:T(128)}, f32[128]{0:T(128)}) all-reduce(f32[128]{0:T(128)S(1)} %get-tuple-element.246, f32[128]{0:T(128)S(1)} %get-tuple-element.257), channel_id=1, replica_groups=mesh['batch'=8,'tensor'=4] {'batch'}, use_global_device_ids=true, to_apply=%region_28.29 | all-reduce | flops 256 | bytes 2048 | tf_op jit(solution)/shard_map/psum | solution.py:239
  460.9 47.7 %all-reduce.9.cloned.1.call-done = f32[2048,512]{1,0:T(8,128)} async-done(((f32[2048,512]{1,0:T(8,128)}), f32[2048,512]{1,0:T(8,128)}) %all-reduce.9.cloned.1.call-update) | async-done | bytes 4194320 | tf_op jit(solution)/shard_map/psum | solution.py:30
  508.7 3.6 multiply_reduce_fusion.4
  512.3 2.9 dynamic-slice_reduce_fusion
  515.5 43.6 %all-reduce = (f32[512]{0:T(512)}, f32[512]{0:T(512)}, f32[512]{0:T(512)}, f32[512]{0:T(512)}, f32[4]{0:T(128)S(1)}) all-reduce(f32[512]{0:T(512)S(1)} %dynamic_update_slice.29, f32[512]{0:T(512)S(1)} %dynamic_update_slice.30, f32[512]{0:T(512)S(1)} %dynamic_update_slice.31, ...), channel_id=1, replica_groups=mesh['batch'=8,'tensor'=4] {'batch','tensor'}, use_global_device_ids=true, to_apply=%region_32.33 | all-reduce | flops 2052 | bytes 16416 | tf_op jit(solution)/shard_map/psum | solution.py:262
  565.5 96.0 %all-reduce.11.cloned.1.call-done = (f32[512,128]{1,0:T(8,128)}, f32[512,128]{1,0:T(8,128)}, f32[512,128]{1,0:T(8,128)}, f32[128,512]{1,0:T(8,128)}, f32[512,512...) async-done(((f32[512,128]{1,0:T(8,128)}, f32[512,128]{1,0:T(8,128)}, f32[512,128]{1,0:T(8,128)}, f32[128,512]{1,0:T(8,128)}, ...) | async-done | bytes 3670032 | tf_op jit(solution)/shard_map/psum | solution.py:239
  (235 shorter events, 103.3 us)
Async XLA Ops:
  7.2 170.6 %copy-start = (bf16[512,512]{1,0:T(8,128)(2,1)S(1)}, bf16[512,512]{1,0:T(8,128)(2,1)}, u32[]{:S(2)}) copy-start(bf16[512,512]{1,0:T(8,128)(2,1)} %param.27) | copy-start | bytes 1572868
  7.2 32.6 %copy-start.52 = (f32[512]{0:T(512)S(1)}, f32[512]{0:T(512)}, u32[]{:S(2)}) copy-start(f32[512]{0:T(512)} %param.32) | copy-start | bytes 6148
  7.2 32.6 %copy-start.54 = (f32[512]{0:T(512)S(1)}, f32[512]{0:T(512)}, u32[]{:S(2)}) copy-start(f32[512]{0:T(512)} %param.33) | copy-start | bytes 6148
  7.2 28.0 %all-gather.5.cloned.1.call-start = ((), (), s32[]{:S(2)}) async-start(), calls=%async_computation.2 | async-start | bytes 2621440 | tf_op jit(solution)/shard_map/all_gather | solution.py:129
  8.0 119.6 %reduce-scatter.3.cloned.1.call-start = ((), (), s32[]{:S(2)}) async-start(), calls=%async_computation.3 | async-start | bytes 5242880 | tf_op jit(solution)/shard_map/reduce_scatter | solution.py:124
  8.0 32.8 %copy-start.36 = (bf16[512,128]{1,0:T(8,128)(2,1)S(1)}, bf16[512,128]{1,0:T(8,128)(2,1)}, u32[]{:S(2)}) copy-start(bf16[512,128]{1,0:T(8,128)(2,1)} %param.23) | copy-start | bytes 393220
  39.8 6.6 copy-start.38
  40.8 86.7 %copy-start.2 = (bf16[2048,512]{1,0:T(8,128)(2,1)}, bf16[2048,512]{1,0:T(8,128)(2,1)S(1)}, u32[]{:S(2)}) copy-start(bf16[2048,512]{1,0:T(8,128)(2,1)S(1)} %add_convert_fusion.1) | copy-start | bytes 6291460
  41.5 9.4 %copy-start.40 = (bf16[512,128]{1,0:T(8,128)(2,1)S(1)}, bf16[512,128]{1,0:T(8,128)(2,1)}, u32[]{:S(2)}) copy-start(bf16[512,128]{1,0:T(8,128)(2,1)} %param.24) | copy-start | bytes 393220
  60.0 20.1 %copy-start.35 = (bf16[128,512]{1,0:T(8,128)(2,1)S(1)}, bf16[128,512]{1,0:T(8,128)(2,1)}, u32[]{:S(2)}) copy-start(bf16[128,512]{1,0:T(8,128)(2,1)} %param.25) | copy-start | bytes 393220
  80.2 47.4 %copy-start.45 = (bf16[512,128]{1,0:T(8,128)(2,1)S(1)}, bf16[512,128]{1,0:T(8,128)(2,1)}, u32[]{:S(2)}) copy-start(bf16[512,128]{1,0:T(8,128)(2,1)} %param.28) | copy-start | bytes 393220
  80.2 47.4 %copy-start.56 = (f32[128]{0:T(128)S(1)}, f32[128]{0:T(128)}, u32[]{:S(2)}) copy-start(f32[128]{0:T(128)} %param.30) | copy-start | bytes 1540
  82.9 83.3 %all-gather.7.cloned.1.call-start = ((), (), s32[]{:S(2)}) async-start(), calls=%async_computation.4 | async-start | bytes 5242880 | tf_op jit(solution)/shard_map/all_gather | solution.py:151
  131.0 40.8 %copy-start.51 = (f32[512]{0:T(512)S(1)}, f32[512]{0:T(512)}, u32[]{:S(2)}) copy-start(f32[512]{0:T(512)} %param.34) | copy-start | bytes 6148
  131.0 40.8 %copy-start.55 = (f32[512]{0:T(512)S(1)}, f32[512]{0:T(512)}, u32[]{:S(2)}) copy-start(f32[512]{0:T(512)} %param.35) | copy-start | bytes 6148
  131.0 95.0 %reduce-scatter.5.cloned.1.call-start = ((), (), s32[]{:S(2)}) async-start(), calls=%async_computation.5 | async-start | bytes 5242880 | tf_op jit(solution)/shard_map/reduce_scatter | solution.py:124
  181.3 44.7 %copy-start.44 = (bf16[512,128]{1,0:T(8,128)(2,1)S(1)}, bf16[512,128]{1,0:T(8,128)(2,1)}, u32[]{:S(2)}) copy-start(bf16[512,128]{1,0:T(8,128)(2,1)} %param.29) | copy-start | bytes 393220
  181.3 44.7 %copy-start.57 = (f32[128]{0:T(128)S(1)}, f32[128]{0:T(128)}, u32[]{:S(2)}) copy-start(f32[128]{0:T(128)} %param.31) | copy-start | bytes 1540
  181.3 72.3 %all-gather.9.cloned.1.call-start = ((), (), s32[]{:S(2)}) async-start(), calls=%async_computation.6 | async-start | bytes 2621440 | tf_op jit(solution)/shard_map/all_gather | solution.py:127
  230.6 118.3 %all-reduce.7.cloned.1.call-start = ((), (), s32[]{:S(2)}) async-start(), calls=%async_computation.7 | async-start | bytes 8388608 | tf_op jit(solution)/shard_map/psum | solution.py:30
  263.3 119.7 %all-gather.11.cloned.1.call-start = ((), (), s32[]{:S(2)}) async-start(), calls=%async_computation.8 | async-start | bytes 2621440 | tf_op jit(solution)/shard_map/all_gather | solution.py:127
  359.8 148.8 %all-reduce.9.cloned.1.call-start = ((), (), s32[]{:S(2)}) async-start(), calls=%async_computation.9 | async-start | bytes 8388608 | tf_op jit(solution)/shard_map/psum | solution.py:30
  365.6 21.9 %copy-start.7 = (bf16[2,1024,2,64]{1,3,2,0:T(8,128)(2,1)S(1)}, bf16[2,1024,2,64]{1,3,2,0:T(8,128)(2,1)}, u32[]{:S(2)}) copy-start(bf16[2,1024,2,64]{1,3,2,0:T(8,128)(2,1)} %get-tuple-element.462) | copy-start | bytes 1572868
  365.6 21.9 %copy-start.13 = (bf16[2,1024,2,64]{1,3,2,0:T(8,128)(2,1)S(1)}, bf16[2,1024,2,64]{1,3,2,0:T(8,128)(2,1)}, u32[]{:S(2)}) copy-start(bf16[2,1024,2,64]{1,3,2,0:T(8,128)(2,1)} %get-tuple-element.472) | copy-start | bytes 1572868
  423.0 238.5 %all-reduce.11.cloned.1.call-start = ((), (), s32[]{:S(2)}) async-start(), calls=%async_computation.10 | async-start | bytes 7340032 | tf_op jit(solution)/shard_map/psum | solution.py:239
  433.1 75.5 %copy-start.48 = (f32[2048]{0:T(1024)S(1)}, f32[2048]{0:T(1024)}, u32[]{:S(2)}) copy-start(f32[2048]{0:T(1024)} %copy-done.47) | copy-start | bytes 24580
  433.1 75.5 %copy-start.50 = (f32[2048]{0:T(1024)S(1)}, f32[2048]{0:T(1024)}, u32[]{:S(2)}) copy-start(f32[2048]{0:T(1024)} %copy-done.49) | copy-start | bytes 24580
  434.6 74.1 %copy-start.6 = (bf16[2048,512]{1,0:T(8,128)(2,1)S(1)}, bf16[2048,512]{1,0:T(8,128)(2,1)}, u32[]{:S(2)}) copy-start(bf16[2048,512]{1,0:T(8,128)(2,1)} %all-gather.5.cloned.1.call-done) | copy-start | bytes 6291460
  512.3 160.7 %copy-start.1 = (bf16[512,512]{1,0:T(8,128)(2,1)S(1)}, bf16[512,512]{1,0:T(8,128)(2,1)}, u32[]{:S(2)}) copy-start(bf16[512,512]{1,0:T(8,128)(2,1)} %param.27) | copy-start | bytes 1572868
  661.5 9.1 %copy-start.32 = (f32[512,512]{1,0:T(8,128)S(1)}, f32[512,512]{1,0:T(8,128)}, u32[]{:S(2)}) copy-start(f32[512,512]{1,0:T(8,128)} %get-tuple-element.425) | copy-start | bytes 3145732
  661.5 10.0 %copy-start.43 = (f32[512,128]{1,0:T(8,128)S(1)}, f32[512,128]{1,0:T(8,128)}, u32[]{:S(2)}) copy-start(f32[512,128]{1,0:T(8,128)} %get-tuple-element.426) | copy-start | bytes 786436
  661.5 10.7 %copy-start.42 = (f32[512,128]{1,0:T(8,128)S(1)}, f32[512,128]{1,0:T(8,128)}, u32[]{:S(2)}) copy-start(f32[512,128]{1,0:T(8,128)} %get-tuple-element.427) | copy-start | bytes 786436
  (40 other events, 105.8 us)
Sparse Core Ops, SparseCore 0:
  9.6 25.5 all-gather.4
  83.0 44.4 reduce-scatter.2
  131.1 35.0 all-gather.6
  181.5 44.5 reduce-scatter.4
  230.7 22.8 all-gather.8
  263.4 85.4 all-reduce.6
  359.9 22.9 all-gather.10
  423.1 85.4 all-reduce.8
  514.5 147.0 all-reduce.10
where the time goes:
time: 689 us; the launch traced here: 680 us
  waiting for transfers between devices  422 us (61%)
  matrix products  82.3 us (12%)
  blocking collectives  65.7 us (10%)
  local copies, waits for them, and re-layouts  45.2 us (7%)
  other arithmetic  43.7 us (6%)
  between operations  19.9 us (3%)
    psum x2, waiting for transfers between devices, norm_backward(): summed = lax.psum(partial_value, 'tensor')  133 us
    psum x1, waiting for transfers between devices, per_device(): lax.psum((query_grad, key_grad, value_grad, output_grad, up_grad, down_gr...  96 us
    reduce_scatter x2, waiting for transfers between devices, branch_total(): lax.psum_scatter(partial_value, 'tensor', scatter_dimension=1, tiled=True)  89 us
    psum x1, blocking collectives, per_device(): lax.psum((local_sums, first_gain_grad, first_shift_grad, second_gain_grad...  43.6 us
    all_gather x2, waiting for transfers between devices, branch_gradient(): return lax.all_gather(piece, 'tensor', axis=1, tiled=True)  40.3 us
    all_gather x1, waiting for transfers between devices, per_device(): middle_rows = lax.all_gather(middle, 'tensor', axis=1, tiled=True)  35.1 us
    all_gather x1, waiting for transfers between devices, per_device(): lax.all_gather(tokens, 'tensor', axis=1, tiled=True).astype(jnp.float32)  27.2 us
    unnamed x122, local copies, waits for them, and re-layouts  26.7 us
  transfers between devices with their start and end apart: 9, of which 9 were waited for; matrix products, arithmetic and copies ran while one was open for 4% of the time, Pallas kernels for 0%

commit v1 on v0

v1 whole, which is shorter than its diff:
```python
import functools
import math

import jax
import jax.numpy as jnp
from jax import lax
from jax.experimental import pallas as pl
from jax.experimental.pallas import tpu as pltpu
from jax.sharding import PartitionSpec as P

F32 = jnp.float32
BF16 = jnp.bfloat16
D = 512
LEN = 1024
OWN = 512
QB = 256
LANE = 128
EPSILON = 1e-05
GELU_C = math.sqrt(2.0 / math.pi)
MESH = pl.DeviceIdType.MESH

DOWN, UP, GATE2, WO, GATE1, QKV, ROWS = 0, 2048, 4096, 4608, 5120, 5632, 7168

ORDER = (
    "down:p3", "do:gate2", "down_a", "hidden:p3", "down:p1", "gate2", "down:p2", "up:p3",
    "hidden:p1", "hidden:t", "down_b", "down:t", "down_b", "down_a", "up_a", "gate2", "up:p1",
    "up_a", "down_a", "hidden:p2", "do:middle", "up:p2", "down_b", "up_b", "up:t", "do:output",
    "up_a", "far:0", "output", "up_b", "down_a", "far:1", "far:2", "output", "down_b", "gate2",
    "up_b", "down_a", "up_a", "far:3", "far:end", "up_b", "gate2", "own:0", "far:project",
    "down_a", "own:1", "down_b", "key", "up_a", "value", "gate2", "output", "up_b", "query",
    "own:2", "up_a", "own:3", "down_b", "own:end", "do:other", "own:project", "up_b", "key",
    "value", "up_a", "query", "down_a", "output", "down_b", "key", "do:own", "gate2", "value",
    "output", "do:norm", "sums", "down_b", "give_in", "up_a", "key", "query", "value", "down_a",
    "output", "up_b", "down_b", "up_a", "key", "sums", "gate2", "give_out", "query", "output",
    "key", "sums", "up_b", "value", "query", "output", "key", "up_a", "value", "query", "down_b",
    "sums", "output", "key",
)


def mm(a, b):
    return jnp.dot(a, b, preferred_element_type=F32)


def mm_nt(a, b):
    return lax.dot_general(a, b, (((1,), (1,)), ((), ())), preferred_element_type=F32)


def mm_tn(a, b):
    return lax.dot_general(a, b, (((0,), (0,)), ((), ())), preferred_element_type=F32)


def at(start, size, step=LANE):
    return pl.ds(pl.multiple_of(start, step), size)


def repeat(start, stop, step):
    for i in range(start, stop):
        step(i)


def colsum(v):
    return jnp.sum(v, axis=0, keepdims=True)


def unit(x):
    centred = x - jnp.mean(x, axis=-1, keepdims=True)
    recip = lax.rsqrt(jnp.mean(centred * centred, axis=-1, keepdims=True) + EPSILON)
    return centred * recip, recip


def layer_kernel(
    nb,
    tok, cot, wq, wk, wv, wo, up, dn, g1, g2, b1, b2, ga1, sh1, ga2, sh2,
    lo, ig, fin_o, small_o,
    xs, n1, n1t, wqkv, wo_f, g1_f, g2_f, up_f, dn_f, bias, cotf, cots, cotr,
    qkv, pr, attw, att, mid, ab, ag, n2, n2t, hid, gp, facc, gfb, gfl, gn2, gm, gab, gal,
    gatt, gaw, dvt, dkt, dqkv, gin, gins, ginr, los, igs,
    gr, l1, lx, fin, sums, smb, sml, smt,
    send_sems, recv_sems, local_sems,
):
    t = lax.axis_index("tensor")
    b = lax.axis_index("batch")
    c = t % 2
    y = t // 2
    p1 = t + 1 - 2 * c
    p2 = t + 2 - 4 * y
    p3 = p1 + 2 - 4 * y
    nbits = nb.bit_length() - 1
    nh = min(3, nbits)
    bits = [(b // (1 << k)) % 2 for k in range(nbits)]
    steps_to = [(1 << k) * (1 - 2 * bits[k]) for k in range(nbits)]
    peers = [b + steps_to[k] for k in range(nbits)]
    cube = [
        (b + sum(steps_to[k] for k in range(nh) if (mask >> k) % 2), t)
        for mask in range(1, 1 << nh)
    ]

    sent = []
    local = []

    def send(src, dst, dev):
        k = len(sent)
        copy = pltpu.make_async_remote_copy(
            src_ref=src, dst_ref=dst, send_sem=send_sems.at[k], recv_sem=recv_sems.at[k],
            device_id=dev, device_id_type=MESH,
        )
        copy.start()
        sent.append(copy)
        return copy

    finished = set()

    def finish(copy):
        if id(copy) not in finished:
            finished.add(id(copy))
            copy.wait_send()

    def fetch(src, dst):
        copy = pltpu.make_async_copy(src, dst, local_sems.at[len(local)])
        copy.start()
        local.append(copy)
        return copy

    d1, d2, d3 = (b, p1), (b, p2), (b, p3)

    win = at(y * LEN, LEN)

    def qkv_blocks(slot):
        return [wqkv.at[:, at(slot * 384 + j * LANE, LANE)] for j in range(3)]

    def mid_blocks(q):
        return [wo_f.at[at(q * LANE, LANE)], g1_f.at[:, at(q * LANE, LANE)]]

    def up_blocks(q):
        return [up_f.at[q], g2_f.at[:, at(q * LANE, LANE)]]

    def piece(ref):
        rows = ref.shape[0] >> min(2, nbits)
        return ref.at[at(sum(bits[k] * (rows << k) for k in range(min(2, nbits))), rows, 32)]

    got_tok = fetch(tok.at[win], xs.at[t])
    got_qkv = [fetch(w, dst) for w, dst in zip((wq, wk, wv), qkv_blocks(y))]
    got_cot = fetch(cot, cotf)
    got_mid = [fetch(w, dst) for w, dst in zip((wo, g1), mid_blocks(t))]
    got_ffn = [fetch(w, dst) for w, dst in zip((up, g2, dn), up_blocks(t) + [dn_f.at[t]])]

    barrier = pltpu.get_barrier_semaphore()
    partners = [d1, d2, d3] + cube + [(peer, t) for peer in peers[nh:]]
    for dev in partners:
        pl.semaphore_signal(barrier, inc=1, device_id=dev, device_id_type=MESH)
    pl.semaphore_wait(barrier, len(partners))

    square = cube[:(1 << min(2, nbits)) - 1]

    def over_y(blocks, refs):
        return [send(piece(w), piece(dst), d2) for w, dst in zip(blocks, refs)]

    def over_square(copies, refs):
        for copy in copies:
            copy.wait_recv()
        return [send(piece(ref), piece(ref), dev) for ref in refs for dev in square]

    def over_core(copies, refs):
        for copy in copies:
            copy.wait_recv()
        return [send(ref, ref, d1) for ref in refs]

    def token_half(i):
        rows = pl.ds(i * OWN, OWN)
        return send(tok.at[at((1 - y) * LEN + i * OWN, OWN)], xs.at[t, rows], d2)

    qkv_y = over_y((wq, wk, wv), qkv_blocks(y))
    tok_2 = [token_half(0), token_half(1)]
    tok_1 = send(tok.at[win], xs.at[t], d1)
    bias[t, 0:1, :] = b1[...]
    bias[t, 1:2, :] = b2[...]
    bias_x = [send(bias.at[t], bias.at[t], dev) for dev in (d1, d2, d3)]
    mid_1 = [send(w, dst, d1) for w, dst in zip((wo, g1), mid_blocks(t))]

    qkv_s = over_square(qkv_y, qkv_blocks(1 - y))
    up_y = over_y((up, g2), up_blocks(t))
    got_cot.wait()

    def to_low(i, carry):
        rows = at(i * QB, QB)
        cots[rows] = cotf[rows].astype(BF16)
        return carry

    lax.fori_loop(0, 4 * OWN // QB, to_low, 0)
    cotr[t] = cots[at(t * OWN, OWN)]
    def pass_tokens(i):
        rows = pl.ds(i * OWN, OWN)
        tok_2[i].wait_recv()
        return send(xs.at[p2, rows], xs.at[p2, rows], d1)

    tok_3 = [pass_tokens(0), pass_tokens(1)]
    mid_y = over_y((wo, g1), mid_blocks(t))
    dn_y = [send(dn, dn_f.at[t], d2)]
    ffn_1 = [send(w, dst, d1) for w, dst in zip((up, g2, dn), up_blocks(t) + [dn_f.at[t]])]

    def tokens_at(rows):
        return jnp.concatenate([xs[j, rows, :].astype(F32) for j in range(4)], axis=1)

    def first_norm(i):
        rows = at(i * QB, QB)
        u, _ = unit(tokens_at(rows))
        n1[rows, :] = (u * ga1[...] + sh1[...]).astype(BF16)

    got_tok.wait()
    tok_1.wait_recv()
    tok_3[0].wait_recv()
    repeat(0, OWN // QB, first_norm)
    up_s = over_square(up_y, up_blocks(p2))
    tok_3[1].wait_recv()
    repeat(OWN // QB, LEN // QB, first_norm)

    for copy in got_qkv:
        copy.wait()
    for copy in qkv_s:
        copy.wait_recv()

    def project(i):
        rows = at(i * QB, QB)
        out = mm(n1[rows, :], wqkv[...])
        for s in range(2):
            base = s * 384
            qkv[rows, base:base + LANE] = (out[:, base:base + LANE].astype(BF16) * 0.125).astype(BF16)
            qkv[rows, base + LANE:base + 384] = out[:, base + LANE:base + 384].astype(BF16)

    repeat(0, LEN // QB, project)

    lane = lax.broadcasted_iota(jnp.int32, (1, LANE), 1)
    heads = [lane < 64, lane >= 64]
    heads_low = [jnp.where(h, 1.0, 0.0).astype(BF16) for h in heads]
    causal = lax.broadcasted_iota(jnp.int32, (QB, QB), 0) >= lax.broadcasted_iota(
        jnp.int32, (QB, QB), 1
    )

    def attend(s):
        base = s * 384
        for i in range(LEN // QB):
            rows = pl.ds(i * QB, QB)
            query = qkv[rows, at(base, LANE)]
            outs = []
            for h in range(2):
                masked = query * heads_low[h]
                near = mm_nt(masked, qkv[rows, at(base + LANE, LANE)])
                near = jnp.where(causal, near, -1e30)
                peak = jnp.max(near, axis=-1, keepdims=True)
                if i > 0:
                    far = mm_nt(masked, qkv[0:i * QB, at(base + LANE, LANE)])
                    peak = jnp.maximum(peak, jnp.max(far, axis=-1, keepdims=True))
                    far = jnp.exp(far - peak)
                near = jnp.exp(near - peak)
                total = jnp.sum(near, axis=-1, keepdims=True)
                if i > 0:
                    total = total + jnp.sum(far, axis=-1, keepdims=True)
                scale = 1.0 / total
                near = (near * scale).astype(BF16)
                pr[s * 2 + h, rows, i * QB:(i + 1) * QB] = near
                out = mm(near, qkv[rows, at(base + 2 * LANE, LANE)])
                if i > 0:
                    far = (far * scale).astype(BF16)
                    pr[s * 2 + h, rows, 0:i * QB] = far
                    out = out + mm(far, qkv[0:i * QB, at(base + 2 * LANE, LANE)])
                outs.append(out)
            attw[rows, at(s * LANE, LANE)] = jnp.where(heads[0], outs[0], outs[1]).astype(BF16)
    own_w = at(c * OWN, OWN)
    other_w = at((1 - c) * OWN, OWN)
    att_x = []
    moved = {"mid": over_square(mid_y, mid_blocks(p2))}

    for s in range(2):
        attend(s)
        cols = at((c + 2 * s) * LANE, LANE)
        att_x.append(send(attw.at[other_w, pl.ds(s * LANE, LANE)], att.at[:, cols], d1))
        att[:, cols] = attw[own_w, pl.ds(s * LANE, LANE)]

    moved["mid"] = over_core(moved["mid"], mid_blocks(p2))
    dn_3 = over_core(dn_y, (dn_f.at[p2],))
    cot_x = [
        send(cots.at[at(p * OWN, OWN)], cotr.at[t], dev)
        for p, dev in ((p1, d1), (p2, d2), (p3, d3))
    ]
    up_3 = over_core(up_s, up_blocks(p2))
    for copy in got_mid:
        copy.wait()
    for copy in mid_1 + moved["mid"] + bias_x + att_x:
        copy.wait_recv()

    sums[...] = jnp.zeros((16, D), F32)

    def note(row, value):
        sums[row:row + 1, :] += value

    def row_of(j):
        return jnp.concatenate([bias[k, j:j + 1, :] for k in range(4)], axis=1)

    def first_branch(i):
        rows = at(i * QB, QB)
        wrows = at(c * OWN + i * QB, QB)
        branch = mm(att[rows, :], wo_f[...])
        gate = jax.nn.sigmoid(mm(n1[wrows, :], g1_f[...]) + row_of(0))
        middle = tokens_at(wrows) + gate * branch
        ab[rows, :] = branch
        ag[rows, :] = gate
        mid[rows, :] = middle
        u, _ = unit(middle)
        n2[rows, :] = (u * ga2[...] + sh2[...]).astype(BF16)
        note(6, colsum(gate))
        note(7, colsum(gate * gate))

    repeat(0, OWN // QB, first_branch)

    for copy in got_ffn:
        copy.wait()

    def forward_up(q):
        for i in range(OWN // QB):
            rows = pl.ds(i * QB, QB)
            pre = mm(n2[rows, :], up_f[q])
            square = pre * pre
            th = jnp.tanh(pre * (GELU_C + (0.044715 * GELU_C) * square))
            share = 0.5 + 0.5 * th
            hidden = pre * share
            hid[q, rows, :] = hidden.astype(BF16)
            tilt = hidden * (1.0 - share)
            slope = share + tilt * (2.0 * GELU_C + (0.26829 * GELU_C) * square)
            gp[q, rows, :] = slope.astype(BF16)

    def forward_down(one, two, first):
        for i in range(OWN // QB):
            rows = pl.ds(i * QB, QB)
            part = mm(hid[one, rows, :], dn_f[one]) + mm(hid[two, rows, :], dn_f[two])
            facc[rows, :] = part if first else facc[rows, :] + part

    forward_up(t)
    for copy in ffn_1:
        copy.wait_recv()
    forward_up(p1)
    forward_down(t, p1, True)
    forward_up(p2)
    for copy in up_3:
        copy.wait_recv()
    forward_up(p3)
    for copy in dn_3:
        copy.wait_recv()
    forward_down(p2, p3, False)

    for copy in cot_x:
        copy.wait_recv()

    def cot_at(rows):
        return jnp.concatenate([cotr[j, rows, :].astype(F32) for j in range(4)], axis=1)

    def second_branch(i):
        rows = at(i * QB, QB)
        branch = facc[rows, :]
        gate = jax.nn.sigmoid(mm(n2[rows, :], g2_f[...]) + row_of(1))
        out = (mid[rows, :] + gate * branch).astype(BF16)
        for j in range(4):
            los[j, rows, :] = out[:, j * LANE:(j + 1) * LANE]
        grad = cot_at(rows)
        gfb[rows, :] = (grad * gate).astype(BF16)
        logit = (grad * branch * gate * (1.0 - gate)).astype(BF16)
        gfl[rows, :] = logit
        note(5, colsum(logit.astype(F32)))
        note(8, colsum(gate))
        note(9, colsum(gate * gate))

    repeat(0, OWN // QB, second_branch)

    mine = at(t * OWN, OWN)

    def give_back(blocks, out):
        fetch(blocks.at[t], out.at[mine])
        return [send(blocks.at[p], out.at[mine], dev) for p, dev in ((p1, d1), (p2, d2), (p3, d3))]

    landing = [0]

    def land(size):
        start = landing[0]
        landing[0] += size
        return start

    def sum_rows(dst, q, base, off, size, terms):
        if not terms:
            return
        chunk = next(n for n in (256, 128, 64) if size % n == 0)

        def step(i, carry):
            here = off + i * chunk
            rows = at(base + here, chunk, 32)
            total = gr[q, rows, :].astype(F32)
            for ref, start in terms:
                total = total + ref[at(start + here, chunk, 32), :].astype(F32)
            dst[rows, :] = total.astype(BF16)
            return carry

        lax.fori_loop(0, size // chunk, step, 0)

    def place(dims, mask):
        return sum(
            (1 << k) * (1 - bits[dim] if (mask >> k) % 2 else bits[dim])
            for k, dim in enumerate(dims)
        )

    def peer_of(dims, mask):
        return (b + sum(steps_to[dim] for k, dim in enumerate(dims) if (mask >> k) % 2), t)

    def reduce_stages(base, size, order, terms):
        off, span = 0, size
        quarters = [("far", p2), ("own", t)]
        for dim in order:
            copies = []
            if dim == "y":
                quarters = quarters[1:]
                sum_rows(gr.at[p2], p2, base, off, span, terms["far"])
                start = land(span)
                rows = at(base + off, span, 32)
                copies.append(send(gr.at[p2, rows], lx.at[pl.ds(start, span)], d2))
                terms["own"] = terms["own"] + [(lx, start - off)]
                yield copies
                continue
            if isinstance(dim, tuple):
                span = span >> len(dim)
                keep = off + place(dim, 0) * span
                for mask in range(1, 1 << len(dim)):
                    away = off + place(dim, mask) * span
                    sum_rows(gr.at[t], t, base, away, span, terms["own"])
                    copies.append((mask, away))
                landed = []
                for k, (mask, away) in enumerate(copies):
                    start = land(span)
                    rows = at(base + away, span, 32)
                    copies[k] = send(gr.at[t, rows], lx.at[pl.ds(start, span)], peer_of(dim, mask))
                    landed.append((lx, start - keep))
                terms["own"] = terms["own"] + landed
                off = keep
                yield copies
                continue
            span = span // 2
            keep = off + bits[dim] * span
            away = off + (1 - bits[dim]) * span
            for name, q in quarters:
                sum_rows(gr.at[q], q, base, away, span, terms[name])
                start = land(span)
                rows = at(base + away, span, 32)
                copies.append(send(gr.at[q, rows], lx.at[pl.ds(start, span)], (peers[dim], t)))
                terms[name] = terms[name] + [(lx, start - keep)]
            off = keep
            yield copies
        for dim in range(nh, nbits):
            sum_rows(gr.at[t], t, base, off, span, terms["own"])
            start = land(span)
            rows = at(base + off, span, 32)
            copy = send(gr.at[t, rows], lx.at[pl.ds(start, span)], (peers[dim], t))
            yield [copy]
            finish(copy)
            terms["own"] = [(lx, start - off)]
        sum_rows(fin, t, base, off, span, terms["own"])
        for dim in reversed([dim for dim in order if dim != "y"]):
            part = fin.at[at(base + off, span, 32)]
            if isinstance(dim, tuple):
                masks = range(1, 1 << len(dim))
                yield [send(part, part, peer_of(dim, mask)) for mask in masks]
                off = off - place(dim, 0) * span
                span = span << len(dim)
                continue
            yield [send(part, part, (peers[dim], t))]
            off = off - bits[dim] * span
            span = span * 2
        fetch(fin.at[pl.ds(base, size)], fin_o.at[pl.ds(base, size)])

    def waiting(stages):
        for copies in stages:
            yield
            for copy in copies:
                copy.wait_recv()

    def batch_order(*dims):
        order = []
        for dim in dims:
            if isinstance(dim, tuple):
                dim = tuple(d for d in dim if d < nh)
                dim = dim if len(dim) > 1 else dim[0] if dim else nh
            if isinstance(dim, tuple) or dim == "y" or dim < nh:
                order.append(dim)
        if dims[0] != "y" and order[0] == "y":
            order[:2] = order[1::-1]
        return order

    def gradient_chain(base, size, order, split):
        rows = pl.ds(base, size)
        far = send(gr.at[p3, rows], l1.at[1, rows], d1)
        if split:
            yield
        y_first = order[0] == "y"
        if y_first and split:
            own = []
        else:
            own = [send(gr.at[p1, rows], l1.at[0, rows], d1)]
            yield
        far.wait_recv()
        if not y_first:
            own[0].wait_recv()
        terms = {"far": [(l1.at[1], base)], "own": [(l1.at[0], base)]}
        stages = waiting(reduce_stages(base, size, order, terms))
        if y_first:
            next(stages)
            yield
            if split:
                own = [send(gr.at[p1, rows], l1.at[0, rows], d1)]
                yield
            own[0].wait_recv()
        yield from stages

    def last_gradients(base, size, order):
        yield from waiting(reduce_stages(base, size, order, {"far": [], "own": []}))

    def sum_chain():
        copies = [
            send(sums.at[:, at(p * LANE, LANE)], sml.at[k], dev)
            for k, (p, dev) in enumerate(((p1, d1), (p2, d2), (p3, d3)))
        ]
        yield
        for copy in copies:
            copy.wait_recv()
        smb[0] = sums[:, at(t * LANE, LANE)] + sml[0] + sml[1] + sml[2]
        copies = [send(smb.at[0], sml.at[3 + k], dev) for k, dev in enumerate(cube)]
        yield
        for copy in copies:
            copy.wait_recv()
        total = smb[0]
        for k in range(len(cube)):
            total = total + sml[3 + k]
        place_now = 3 + len(cube)
        for k in range(nh, nbits):
            smb[k - nh + 1] = total
            copy = send(smb.at[k - nh + 1], sml.at[place_now], (peers[k], t))
            yield
            copy.wait_recv()
            total = total + sml[place_now]
            place_now += 1
        smt[t] = total
        copies = [send(smt.at[t], smt.at[t], dev) for dev in (d1, d2, d3)]
        yield
        for copy in copies:
            copy.wait_recv()
        fetch(smt, small_o)

    returned = []

    def give_chain(blocks, out):
        returned.extend(give_back(blocks, out))
        yield

    chains = {
        "down_a": gradient_chain(DOWN, 1024, batch_order("y", 0, (1, 2)), True),
        "down_b": gradient_chain(DOWN + 1024, 1024, batch_order(0, "y", 1, 2), True),
        "up_a": gradient_chain(UP, 1024, batch_order(1, "y", 0, 2), True),
        "up_b": gradient_chain(UP + 1024, 1024, batch_order("y", 0, (1, 2)), True),
        "gate2": gradient_chain(GATE2, D, batch_order(0, "y", (1, 2)), False),
        "output": gradient_chain(WO, QKV - WO, batch_order(1, 0, "y", 2), False),
        "query": last_gradients(QKV, D, batch_order("y", 0, (1, 2))),
        "key": last_gradients(QKV + D, D, batch_order("y", 0, 1, 2)),
        "value": last_gradients(QKV + 2 * D, D, batch_order("y", (0, 1), 2)),
        "sums": sum_chain(),
        "give_out": give_chain(los, lo),
        "give_in": give_chain(igs, ig),
    }

    def gradient_rows(q, base, i, grad):
        for j in range(grad.shape[1] // LANE):
            gr[q, pl.ds(base + j * D + i * QB, QB), :] = grad[:, j * LANE:(j + 1) * LANE]

    def down_gradient(q):
        for i in range(2):
            grad = mm_tn(hid[q, :, i * QB:(i + 1) * QB], gfb[...]).astype(BF16)
            gradient_rows(q, DOWN, i, grad)

    done = set()

    def once(name):
        new = name not in done
        done.add(name)
        return new

    def turn_second():
        if once("n2t"):
            n2t[...] = n2[...].T

    def turn_first():
        if once("n1t"):
            for i in range(LEN // QB):
                n1t[:, i * QB:(i + 1) * QB] = n1[i * QB:(i + 1) * QB, :].T

    def hidden_back(q):
        first = once("gn2")
        for i in range(OWN // QB):
            rows = pl.ds(i * QB, QB)
            grad = mm_nt(gfb[rows, :], dn_f[q])
            pre = (grad * gp[q, rows, :].astype(F32)).astype(BF16)
            gp[q, rows, :] = pre
            part = mm_nt(pre, up_f[q])
            gn2[rows, :] = part if first else gn2[rows, :] + part

    def up_gradient(q):
        turn_second()
        for i in range(2):
            gradient_rows(q, UP, i, mm(n2t[i * QB:(i + 1) * QB, :], gp[q]).astype(BF16))

    def gate_gradient(left, right, base):
        for i in range(2):
            grad = mm(left(slice(i * QB, (i + 1) * QB)), right[...]).astype(BF16)
            for j in range(4):
                gr[j, pl.ds(base + i * QB, QB), :] = grad[:, j * LANE:(j + 1) * LANE]

    def second_gate_gradient():
        turn_second()
        gate_gradient(lambda cols: n2t[cols, :], gfl, GATE2)

    def second_back(i):
        rows = at(i * QB, QB)
        grad = gn2[rows, :] + mm_nt(gfl[rows, :], g2_f[...])
        u, recip = unit(mid[rows, :])
        s = grad * ga2[...]
        through = recip * (
            s - jnp.mean(s, axis=-1, keepdims=True) - u * jnp.mean(s * u, axis=-1, keepdims=True)
        )
        total = cot_at(rows) + through
        gm[rows, :] = total
        note(2, colsum(grad * u))
        note(3, colsum(grad))
        gate = ag[rows, :]
        low = (total * gate).astype(BF16)
        gab[rows, :] = low
        logit = (total * ab[rows, :] * gate * (1.0 - gate)).astype(BF16)
        gal[rows, :] = logit
        note(4, colsum(logit.astype(F32)))
        gatt[rows, :] = mm_nt(low, wo_f[...]).astype(BF16)

    exchanged = {}

    def middle_back():
        repeat(0, OWN // QB, second_back)
        for name, q, slot in (("far", p3, 1 - y), ("own", p1, y)):
            exchanged[name] = send(
                gatt.at[:, at(q * LANE, LANE)], gaw.at[own_w, at(slot * LANE, LANE)], d1
            )
        for q, slot in ((p2, 1 - y), (t, y)):
            gaw[own_w, at(slot * LANE, LANE)] = gatt[:, at(q * LANE, LANE)]

    def output_gradient():
        turn_first()
        gate_gradient(lambda cols: n1t[cols, own_w], gal, GATE1)
        for i in range(2):
            outer = mm_tn(att[:, i * QB:(i + 1) * QB], gab[...]).astype(BF16)
            for k in range(2):
                for j in range(4):
                    gr[2 * i + k, pl.ds(WO + j * LANE, LANE), :] = outer[
                        k * LANE:(k + 1) * LANE, j * LANE:(j + 1) * LANE
                    ]

    slots = {"far": 1 - y, "own": y}

    def block_back(name, i):
        if i == 0:
            exchanged[name].wait_recv()
        s = slots[name]
        base = s * 384
        rows = pl.ds(i * QB, QB)
        reach = (i + 1) * QB
        query = qkv[rows, at(base, LANE)]
        grad = gaw[rows, at(s * LANE, LANE)]
        prod = grad.astype(F32) * attw[rows, at(s * LANE, LANE)].astype(F32)
        outs = []
        for h in range(2):
            masked = grad * heads_low[h]
            delta = jnp.sum(jnp.where(heads[h], prod, 0.0), axis=-1, keepdims=True)
            probs = pr[s * 2 + h, rows, 0:reach]
            dprobs = mm_nt(masked, qkv[0:reach, at(base + 2 * LANE, LANE)])
            scores = (probs.astype(F32) * (dprobs - delta)).astype(BF16)
            outs.append(mm(scores, qkv[0:reach, at(base + LANE, LANE)]))
            value_part = mm_tn(masked, probs)
            key_part = mm_tn(query * heads_low[h], scores)
            if h == 0:
                dvt[:, i * QB:reach] = value_part[:, i * QB:reach]
                dkt[:, i * QB:reach] = key_part[:, i * QB:reach]
                if i > 0:
                    dvt[:, 0:i * QB] += value_part[:, 0:i * QB]
                    dkt[:, 0:i * QB] += key_part[:, 0:i * QB]
            else:
                dvt[:, 0:reach] += value_part
                dkt[:, 0:reach] += key_part
        dqkv[rows, at(base, LANE)] = (jnp.where(heads[0], outs[0], outs[1]) * 0.125).astype(BF16)

    def blocks_end(name):
        base = slots[name] * 384
        for i in range(LEN // QB):
            rows = pl.ds(i * QB, QB)
            dqkv[rows, at(base + LANE, LANE)] = dkt[:, i * QB:(i + 1) * QB].T.astype(BF16)
            dqkv[rows, at(base + 2 * LANE, LANE)] = dvt[:, i * QB:(i + 1) * QB].T.astype(BF16)

    def project_back(name):
        turn_first()
        q = {"far": p2, "own": t}[name]
        for i in range(2):
            grad = mm(n1t[i * QB:(i + 1) * QB, :], dqkv[:, at(slots[name] * 384, 384)])
            gradient_rows(q, QKV, i, grad.astype(BF16))

    def back_to_other():
        for i in range(OWN // QB):
            rows = at((1 - c) * OWN + i * QB, QB)
            gins[pl.ds(i * QB, QB), :] = mm_nt(dqkv[rows, :], wqkv[...]).astype(BF16)
        exchanged["in"] = send(gins, ginr, d1)

    def back_to_own():
        for i in range(OWN // QB):
            rows = pl.ds(i * QB, QB)
            gin[rows, :] = mm_nt(dqkv[at(c * OWN + i * QB, QB), :], wqkv[...]) + mm_nt(
                gal[rows, :], g1_f[...]
            )

    def first_back(i):
        rows = at(i * QB, QB)
        grad = gin[rows, :] + ginr[rows, :].astype(F32)
        u, recip = unit(tokens_at(at(c * OWN + i * QB, QB)))
        s = grad * ga1[...]
        through = recip * (
            s - jnp.mean(s, axis=-1, keepdims=True) - u * jnp.mean(s * u, axis=-1, keepdims=True)
        )
        total = (gm[rows, :] + through).astype(BF16)
        for j in range(4):
            igs[j, rows, :] = total[:, j * LANE:(j + 1) * LANE]
        note(0, colsum(grad * u))
        note(1, colsum(grad))

    def norm_back():
        exchanged["in"].wait_recv()
        repeat(0, OWN // QB, first_back)

    quarters = {"p3": p3, "p2": p2, "p1": p1, "t": t}
    steps = {
        "gate2": second_gate_gradient, "middle": middle_back, "output": output_gradient,
        "other": back_to_other, "own": back_to_own, "norm": norm_back,
    }

    def compute(kind, what):
        if kind == "do":
            steps[what]()
        elif kind in slots:
            if what == "end":
                blocks_end(kind)
            elif what == "project":
                project_back(kind)
            else:
                block_back(kind, int(what))
        else:
            {"down": down_gradient, "hidden": hidden_back, "up": up_gradient}[kind](quarters[what])

    drained = [0]

    def drain(keep):
        while drained[0] < len(sent) - keep:
            finish(sent[drained[0]])
            drained[0] += 1

    def stage(name):
        if name in chains and next(chains[name], 0) == 0:
            del chains[name]
        drain(32)

    for name in ORDER:
        if ":" in name:
            compute(*name.split(":"))
        else:
            stage(name)
    while chains:
        for name in tuple(chains):
            stage(name)
    for copy in returned:
        copy.wait_recv()
    drain(0)
    for copy in local[10:]:
        copy.wait()


def spread_kernel(
    entries, lo, ig, fin, small,
    layer_output, input_gradient, query, key, value, output, upg, downg, gate1, gate2,
    bias1, bias2, gain1, shift1, gain2, shift2, stats,
    lo_v, ig_v, fin_v, small_v, ig_w, square_w, output_w, cols_w, bias_w, norm_w, stats_w,
    sems, out_sems,
):
    t = lax.axis_index("tensor")

    def pull(src, dst, k):
        copy = pltpu.make_async_copy(src, dst, sems.at[k])
        copy.start()
        return copy

    got_small = pull(small, small_v, 6)
    rows = [(DOWN, 2048), (UP, 2048), (GATE2, QKV - GATE2), (QKV, ROWS - QKV)]
    pieces = [
        pull(fin.at[pl.ds(r, n)], fin_v.at[pl.ds(r, n)], 1 + k) for k, (r, n) in enumerate(rows)
    ]
    got_ig = pull(ig, ig_v, 5)
    got_lo = pull(lo, lo_v, 0)
    pushed = []

    def push(src, dst):
        copy = pltpu.make_async_copy(src, dst, out_sems.at[len(pushed)])
        copy.start()
        pushed.append(copy)

    got_small.wait()
    for k, out in enumerate((bias1, bias2)):
        bias_w[k] = small_v[t, 4 + k:5 + k, :]
        push(bias_w.at[k], out)
    for row, out in enumerate((gain1, shift1, gain2, shift2)):
        for j in range(4):
            norm_w[row, :, j * LANE:(j + 1) * LANE] = small_v[j, row:row + 1, :]
        push(norm_w.at[row], out)
    means = [
        jnp.sum(sum(small_v[j, row:row + 1, :] for j in range(4)), axis=1, keepdims=True) / entries
        for row in range(6, 10)
    ]
    lane = lax.broadcasted_iota(jnp.int32, (1, LANE), 1)
    parts = [means[0], means[1] - means[0] * means[0], means[2], means[3] - means[2] * means[2]]
    row = jnp.zeros((1, LANE), F32)
    for j in range(4):
        row = jnp.where(lane == j, parts[j], row)
    stats_w[...] = row[:, 0:4]
    push(stats_w, stats)
    for k, (base, out) in enumerate(((DOWN, downg), (UP, upg))):
        pieces[k].wait()
        for j in range(4):
            square_w[k, :, j * LANE:(j + 1) * LANE] = fin_v[
                base + j * D:base + (j + 1) * D, :
            ].astype(F32)
        push(square_w.at[k], out)
    pieces[2].wait()
    for j in range(4):
        output_w[:, j * LANE:(j + 1) * LANE] = fin_v[
            WO + j * LANE:WO + (j + 1) * LANE, :
        ].astype(F32)
    push(output_w, output)
    for k, (base, out) in enumerate(
        ((GATE2, gate2), (GATE1, gate1), (QKV, query), (QKV + D, key), (QKV + 2 * D, value))
    ):
        if k == 2:
            pieces[3].wait()
        cols_w[k] = fin_v[base:base + D, :].astype(F32)
        push(cols_w.at[k], out)
    got_ig.wait()
    for k in range(2):
        half = pl.ds(k * 2 * OWN, 2 * OWN)
        ig_w[half, :] = ig_v[half, :].astype(F32)
        push(ig_w.at[half], input_gradient.at[half])
    got_lo.wait()
    push(lo_v, layer_output)
    for copy in pushed:
        copy.wait()


def per_device(
    nb, tokens, cotangent, query_weight, key_weight, value_weight, output_weight, up_weight,
    down_weight, first_gate, second_gate, first_bias, second_bias, first_gain, first_shift,
    second_gain, second_shift,
):
    nbits = nb.bit_length() - 1
    nh = min(3, nbits)
    land_rows = 2 * ROWS + (nbits - nh) * (ROWS >> nh)
    sds = jax.ShapeDtypeStruct
    hbm = pl.BlockSpec(memory_space=pl.ANY)
    vmem = pl.BlockSpec(memory_space=pltpu.VMEM)

    def low(*shape):
        return pltpu.VMEM(shape, BF16)

    def full(*shape):
        return pltpu.VMEM(shape, F32)

    scratch = [
        low(4, LEN, LANE),
        low(LEN, D), low(D, LEN),
        low(D, 768),
        low(D, D), low(D, D), low(D, D),
        low(4, D, D), low(4, D, D),
        full(4, 8, LANE),
        full(4 * OWN, LANE),
        low(4 * OWN, LANE), low(4, OWN, LANE),
        low(LEN, 768),
        low(4, LEN, LEN),
        low(LEN, 2 * LANE), low(OWN, D),
        full(OWN, D), full(OWN, D), full(OWN, D),
        low(OWN, D), low(D, OWN),
        low(4, OWN, D), low(4, OWN, D),
        full(OWN, D),
        low(OWN, D), low(OWN, D),
        full(OWN, D), full(OWN, D),
        low(OWN, D), low(OWN, D),
        low(OWN, D), low(LEN, 2 * LANE),
        full(LANE, LEN), full(LANE, LEN),
        low(LEN, 768),
        full(OWN, D), low(OWN, D), low(OWN, D),
        low(4, OWN, LANE), low(4, OWN, LANE),
        low(4, ROWS, LANE),
        low(2, QKV, LANE), low(land_rows, LANE),
        low(ROWS, LANE),
        full(16, D), full(1 + nbits - nh, 16, LANE),
        full(2 + (1 << nh) + nbits - nh, 16, LANE), full(4, 16, LANE),
        pltpu.SemaphoreType.DMA((224,)),
        pltpu.SemaphoreType.DMA((224,)),
        pltpu.SemaphoreType.DMA((32,)),
    ]
    lo, ig, fin, small = pl.pallas_call(
        functools.partial(layer_kernel, nb),
        out_shape=[
            sds((4 * OWN, LANE), BF16), sds((4 * OWN, LANE), BF16),
            sds((ROWS, LANE), BF16), sds((4, 16, LANE), F32),
        ],
        in_specs=[hbm] * 10 + [vmem] * 6,
        out_specs=[hbm] * 4,
        scratch_shapes=scratch,
        compiler_params=pltpu.CompilerParams(
            collective_id=0, has_side_effects=True, vmem_limit_bytes=63 * 1024 * 1024
        ),
    )(
        tokens, cotangent, query_weight, key_weight, value_weight, output_weight, up_weight,
        down_weight, first_gate, second_gate, first_bias.reshape(1, LANE),
        second_bias.reshape(1, LANE), first_gain.reshape(1, D), first_shift.reshape(1, D),
        second_gain.reshape(1, D), second_shift.reshape(1, D),
    )
    entries = float(nb * 4 * OWN * D)
    outs = pl.pallas_call(
        functools.partial(spread_kernel, entries),
        out_shape=[
            sds((4 * OWN, LANE), BF16), sds((4 * OWN, LANE), F32),
            sds((D, LANE), F32), sds((D, LANE), F32), sds((D, LANE), F32),
            sds((LANE, D), F32), sds((D, D), F32), sds((D, D), F32),
            sds((D, LANE), F32), sds((D, LANE), F32),
            sds((1, LANE), F32), sds((1, LANE), F32),
            sds((1, D), F32), sds((1, D), F32), sds((1, D), F32), sds((1, D), F32),
            sds((1, 4), F32),
        ],
        in_specs=[hbm] * 4,
        out_specs=[hbm] * 17,
        scratch_shapes=[
            low(4 * OWN, LANE), low(4 * OWN, LANE), low(ROWS, LANE), full(4, 16, LANE),
            full(4 * OWN, LANE), full(2, D, D), full(LANE, D), full(5, D, LANE),
            full(2, 1, LANE), full(4, 1, D), full(1, 4),
            pltpu.SemaphoreType.DMA((8,)), pltpu.SemaphoreType.DMA((24,)),
        ],
        compiler_params=pltpu.CompilerParams(vmem_limit_bytes=63 * 1024 * 1024),
    )(lo, ig, fin, small)
    return tuple(outs[:10]) + (
        outs[10].reshape(LANE), outs[11].reshape(LANE), outs[12].reshape(D),
        outs[13].reshape(D), outs[14].reshape(D), outs[15].reshape(D), outs[16].reshape(4),
    )


def solution(mesh):
    cols = P(None, "tensor")
    rows = P("tensor", None)
    both = P("batch", "tensor")
    part = P("tensor")
    in_specs = (
        both, both, cols, cols, cols, rows, cols, rows, cols, cols, part, part, P(), P(), P(), P(),
    )
    out_specs = (
        both, both, cols, cols, cols, rows, cols, rows, cols, cols, part, part,
        P(), P(), P(), P(), P(),
    )
    return jax.shard_map(
        functools.partial(per_device, mesh.shape["batch"]),
        mesh=mesh, in_specs=in_specs, out_specs=out_specs, check_vma=False,
    )
```

time: 689 us -> 109 us (0.16); the launches traced: 680 us -> 108 us
  waiting for transfers between devices: 422 us -> 0 us
  Pallas kernels: 0 us -> 108 us
  matrix products: 82.3 us -> 0 us
  blocking collectives: 65.7 us -> 0 us
  local copies, waits for them, and re-layouts: 45.2 us -> 0 us
  other arithmetic: 43.7 us -> 0 us
  between operations: 19.9 us -> 0.85 us
    psum x3 -> x0, waiting for transfers between devices: 229 us -> none  [the longest x2 133 us: norm_backward(): summed = lax.psum(partial_value, 'tensor')]
    pallas_call x0 -> x2, Pallas kernels: none -> 108 us  [the longest x1 104 us: per_device(): pl.pallas_call(functools.partial(layer_kernel, nb), out_shape=[sds((4 * O...]
    all_gather x4 -> x0, waiting for transfers between devices: 103 us -> none  [the longest x2 40.3 us: branch_gradient(): return lax.all_gather(piece, 'tensor', axis=1, tiled=True)]
    reduce_scatter x2 -> x0, waiting for transfers between devices: 89 us -> none  [branch_total(): lax.psum_scatter(partial_value, 'tensor', scatter_dimension=1, tiled=True)]
    dot_general x38 -> x0, matrix products: 82.3 us -> none  [the longest x4 8.28 us: scores_of(): jnp.einsum('qhd,khd->hqk', query_rows, key_rows, preferred_element_type=j...]
    psum x2 -> x0, blocking collectives: 65.7 us -> none  [the longest x1 43.6 us: per_device(): lax.psum((local_sums, first_gain_grad, first_shift_grad, second_gain_grad...]
    reduce_sum x10 -> x0, other arithmetic: 29.5 us -> none  [the longest x2 7.91 us: norm_backward(): first_mean = jnp.mean(scaled_full, axis=-1, keepdims=True)]
    unnamed x122 -> x0, local copies, waits for them, and re-layouts: 26.7 us -> none
  transfers between devices with their start and end apart: 9 -> 0, of which waited for: 9 -> 0; matrix products, arithmetic and copies ran while one was open for 4% -> 0% of each run, Pallas kernels for 0% -> 0%
where the time goes in v1:
time: 109 us; the launch traced here: 108 us
  Pallas kernels  108 us (99%)
    pallas_call x1, Pallas kernels, per_device(): pl.pallas_call(functools.partial(layer_kernel, nb), out_shape=[sds((4 * O...  104 us
    pallas_call x1, Pallas kernels, per_device(): pl.pallas_call(functools.partial(spread_kernel, entries), out_shape=[sds(...  3.82 us

profile of v1, /device:TPU:0, one launch (start us, length us, event | category | flops | bytes accessed | tf_op | source)
XLA Modules:
  0.0 108.4 jit_solution(3049196011248089567)
XLA Ops:
  0.7 103.7 %shard_map.287 = (bf16[2048,128]{1,0:T(8,128)(2,1)}, bf16[2048,128]{1,0:T(8,128)(2,1)}, bf16[7168,128]{1,0:T(8,128)(2,1)}, f32[4,16,128]{2,1,0:T(8,128)}) custom-call(bf16[2048,128]{1,0:T(8,128)(2,1)} %tok.1, f32[2048,128]{1,0:T(8,128)} %cot.1, bf16[512,128]{1,0:T(8,128)(2,1)} %wq.1, bf16[512,128]{1,0:T(8,128)(2,1)} %wk.1, bf16[512,128]{1,0:T(8,128)(2,1)} %wv.1, ...), custom_call_target="tpu_custom_call" | custom-call | tf_op jit(solution)/shard_map/pallas_call | solution.py:918
  104.4 3.8 %shard_map.288 = (bf16[2048,128]{1,0:T(8,128)(2,1)}, f32[2048,128]{1,0:T(8,128)}, f32[512,128]{1,0:T(8,128)}, f32[512,128]{1,0:T(8,128)}, f32[512,128]{1,0:T(8,1...) custom-call(bf16[2048,128]{1,0:T(8,128)(2,1)} %get-tuple-element.38., ...), custom_call_target="tpu_custom_call" | custom-call | tf_op jit(solution)/shard_map/pallas_call | solution.py:937
